TPU v7x, 32 devices: a whole 2x2x4 slice. The times are simulated.
32 devices in a mesh: row: 8 (over z, x), col: 4 (over y, core).
Axes of the slice: x: 2, y: 2, z: 4, core: 2. Of those that a mesh axis runs over, the one named last changes fastest.
Arguments:
- tokens: bfloat16 [80, 8192], P('row', 'col'), may hold values from -6 to 6
- w_gate: bfloat16 [8192, 16384], P('row', 'col'), may hold values from -0.0625 to 0.0625
- w_up: bfloat16 [8192, 16384], P('row', 'col'), may hold values from -0.0625 to 0.0625
- w_down: bfloat16 [16384, 8192], P('row', 'col'), may hold values from -0.046875 to 0.046875
- out_grad: bfloat16 [80, 8192], P('row', 'col'), may hold values from -4 to 4
Outputs:
- output: bfloat16 [80, 8192], P('row', 'col')
- grad_tokens: bfloat16 [80, 8192], P('row', 'col')
- grad_gate: bfloat16 [8192, 16384], P('row', 'col')
- grad_up: bfloat16 [8192, 16384], P('row', 'col')
- grad_down: bfloat16 [16384, 8192], P('row', 'col')
All inputs are finite; a program needn't handle non-finite values.
Results may differ from a plain program's by a relative error of at most 0.0051.
Values may be sent and summed in bfloat16 or wider, within the bound.
A program may use at most 128 MiB of HBM per device.

v0:
```python
import jax
import jax.numpy as jnp
from jax import lax
from jax.sharding import PartitionSpec as P

rows_contract = (((0,), (0,)), ((), ()))
cols_contract = (((1,), (1,)), ((), ()))


def broadcast(x, axis, root):
    mine = lax.axis_index(axis) == root
    return lax.psum(jnp.where(mine, x, jnp.zeros_like(x)), axis)


def per_device(tokens, w_gate, w_up, w_down, out_grad):
    row_index = lax.axis_index("row")
    col_index = lax.axis_index("col")
    tok_rows = tokens.shape[0]
    ff_cols = w_gate.shape[1]
    tokens_all, cotangent_all = (
        lax.all_gather(tokens, "row", axis=0, tiled=True),
        lax.all_gather(out_grad, "row", axis=0, tiled=True),
    )

    def to_row_blocks(matrix):
        piece_cols = matrix.shape[1] // 2
        picked = lax.dynamic_slice_in_dim(matrix, row_index % 2 * piece_cols, piece_cols, 1)
        return broadcast(picked, "col", row_index // 2)

    def to_col_blocks(matrix):
        pieces = []
        for offset in range(2):
            pieces.append(broadcast(matrix, "row", 2 * col_index + offset))
        return jnp.concatenate(pieces, axis=1)

    def col_total(matrix):
        return lax.psum(matrix, "col")

    tokens_rows = to_row_blocks(tokens_all)
    block = tokens_rows
    gate_up = lax.psum_scatter(
        jnp.concatenate(
            [
                jnp.dot(block, w_gate, preferred_element_type=jnp.float32),
                jnp.dot(block, w_up, preferred_element_type=jnp.float32),
            ],
            axis=1,
        ),
        "row",
        scatter_dimension=0,
        tiled=True,
    )
    gate = gate_up[:, :ff_cols]
    up = gate_up[:, ff_cols:]
    sigmoid_gate = jax.nn.sigmoid(gate)
    activated = gate * sigmoid_gate
    hidden_share = (activated * up).astype(jnp.bfloat16)
    hidden_all = lax.all_gather(hidden_share, "row", axis=0, tiled=True)
    hidden_rows = to_row_blocks(hidden_all)
    block = hidden_rows
    output = lax.psum_scatter(
        jnp.dot(block, w_down, preferred_element_type=jnp.float32),
        "row",
        scatter_dimension=0,
        tiled=True,
    ).astype(jnp.bfloat16)
    grad_down = lax.dot_general(
        hidden_rows, cotangent_all, rows_contract, preferred_element_type=jnp.float32
    ).astype(jnp.bfloat16)
    hidden_part = lax.dot_general(
        cotangent_all, w_down, cols_contract, preferred_element_type=jnp.float32
    )
    grad_hidden = to_col_blocks(col_total(hidden_part))
    grad_share = lax.dynamic_slice_in_dim(grad_hidden, row_index * tok_rows, tok_rows, 0)
    gate_term = (grad_share * up * sigmoid_gate * (1.0 + gate * (1.0 - sigmoid_gate))).astype(
        jnp.bfloat16
    )
    up_term = (grad_share * activated).astype(jnp.bfloat16)
    gate_grads, up_grads = (
        lax.all_gather(gate_term, "row", axis=0, tiled=True),
        lax.all_gather(up_term, "row", axis=0, tiled=True),
    )
    grad_gate = lax.dot_general(
        tokens_rows, gate_grads, rows_contract, preferred_element_type=jnp.float32
    ).astype(jnp.bfloat16)
    grad_up = lax.dot_general(
        tokens_rows, up_grads, rows_contract, preferred_element_type=jnp.float32
    ).astype(jnp.bfloat16)
    input_part = lax.dot_general(
        gate_grads, w_gate, cols_contract, preferred_element_type=jnp.float32
    ) + lax.dot_general(up_grads, w_up, cols_contract, preferred_element_type=jnp.float32)
    input_cols = to_col_blocks(col_total(input_part))
    grad_tokens = lax.dynamic_slice_in_dim(input_cols, row_index * tok_rows, tok_rows, 0).astype(
        jnp.bfloat16
    )
    return (output, grad_tokens, grad_gate, grad_up, grad_down)


def solution(mesh):
    in_specs = (P("row", "col"), P("row", "col"), P("row", "col"), P("row", "col"), P("row", "col"))
    out_specs = (
        P("row", "col"),
        P("row", "col"),
        P("row", "col"),
        P("row", "col"),
        P("row", "col"),
    )
    return jax.shard_map(
        per_device, mesh=mesh, in_specs=in_specs, out_specs=out_specs, check_vma=False
    )
```

profile of v0, /device:TPU:0, one launch (start us, length us, event | category | flops | bytes accessed | tf_op | source)
XLA Modules:
  0.0 504.6 jit_solution(4869953054068002365)
XLA Ops:
  7.2 0.0 all-reduce.11.cloned.1.call-start
  7.2 33.2 %all-gather = bf16[8,10,2048]{2,1,0:T(8,128)(2,1)S(1)} all-gather(bf16[1,10,2048]{2,1,0:T(8,128)(2,1)} %bitcast.27), channel_id=1, replica_groups=mesh['row'=8,'col'=4] {'row'}, dimensions={0}, use_global_device_ids=true | all-gather | bytes 368640 | tf_op jit(solution)/shard_map/all_gather | solution.py:21
  40.5 0.1 reshape.11
  40.6 0.7 dynamic-slice_select_fusion.1
  41.3 0.0 all-reduce.11.cloned.1.call-update
  41.3 0.0 all-reduce.15.cloned.1.call-start
  41.4 31.5 %all-gather.2 = bf16[8,10,2048]{2,1,0:T(8,128)(2,1)S(1)} all-gather(bf16[1,10,2048]{2,1,0:T(8,128)(2,1)} %bitcast.28), channel_id=1, replica_groups=mesh['row'=8,'col'=4] {'row'}, dimensions={0}, use_global_device_ids=true | all-gather | bytes 368640 | tf_op jit(solution)/shard_map/all_gather | solution.py:22
  72.9 0.1 reshape.15
  73.0 6.9 %fusion.10 = f32[80,2048]{1,0:T(8,128)} fusion(bf16[80,2048]{1,0:T(8,128)(2,1)S(1)} %reshape.15, bf16[2048,2048]{1,0:T(8,128)(2,1)} %param.8), kind=kOutput, calls=%fused_computation.30 | convolution fusion | flops 671088640 | bytes 9371648 | tf_op jit(solution)/shard_map/dot_general | solution.py:70
  79.9 0.0 all-reduce.15.cloned.1.call-update
  79.9 0.0 all-reduce.19.cloned.1.call-start
  80.0 0.0 all-reduce.11.cloned.1.call-done
  80.0 0.0 copy-start
  80.0 5.1 %fusion.8 = f32[80,4096]{1,0:T(8,128)S(1)} fusion(bf16[80,1024]{1,0:T(8,128)(2,1)} %all-reduce.11.cloned.1.call-done, bf16[1024,4096]{1,0:T(8,128)(2,1)} %param.7), kind=kOutput, calls=%fused_computation.28 | convolution fusion | flops 671088640 | bytes 9863168 | tf_op jit(solution)/shard_map/dot_general | solution.py:45
  85.1 0.0 copy-done
  85.1 5.1 %fusion.7 = f32[80,4096]{1,0:T(8,128)S(1)} fusion(bf16[80,1024]{1,0:T(8,128)(2,1)S(1)} %copy-done, bf16[1024,4096]{1,0:T(8,128)(2,1)} %param.6), kind=kOutput, calls=%fused_computation.27 | convolution fusion | flops 671088640 | bytes 9863168 | tf_op jit(solution)/shard_map/dot_general | solution.py:44
  90.2 0.0 copy-start.2
  90.2 1.7 pad_maximum_fusion
  91.9 23.2 %all-reduce.15.cloned.1.call-done = f32[80,2048]{1,0:T(8,128)} async-done(((f32[80,2048]{1,0:T(8,128)}), f32[80,2048]{1,0:T(8,128)}) %all-reduce.15.cloned.1.call-update) | async-done | bytes 655376 | tf_op jit(solution)/shard_map/psum | solution.py:37
  115.0 2.3 broadcast_select_fusion.1
  117.3 0.0 all-reduce.19.cloned.1.call-update
  117.3 0.0 all-reduce.13.cloned.1.call-start
  117.4 0.0 copy-done.2
  117.4 0.6 dynamic-slice
  118.7 151.4 %all-reduce.19.cloned.1.call-done = (f32[80,8192]{1,0:T(8,128)}, f32[80,2048]{1,0:T(8,128)}, f32[80,2048]{1,0:T(8,128)}) async-done(((f32[80,8192]{1,0:T(8,128)}, f32[80,2048]{1,0:T(8,128)}, f32[80,2048]{1,0:T(8,128)}), (f32[80,8192]{1,0:T(8,128)}, f32[80,2048]{1,0:T(8,128)}, f32[80,2048]{1,0:T(8,128)})) %all-reduce.19.cloned.1.call-update) | async-done | bytes 3932176
  270.0 1.6 fusion.3
  271.6 32.7 %all-gather.1 = bf16[8,10,4096]{2,1,0:T(8,128)(2,1)S(1)} all-gather(bf16[1,10,4096]{2,1,0:T(8,128)(2,1)S(1)} %get-tuple-element.13), channel_id=1, replica_groups=mesh['row'=8,'col'=4] {'row'}, dimensions={0}, use_global_device_ids=true | all-gather | bytes 737280 | tf_op jit(solution)/shard_map/all_gather | solution.py:58
  304.4 0.2 reshape.13
  304.6 0.8 dynamic-slice_select_fusion
  305.4 0.0 all-reduce.13.cloned.1.call-update
  305.4 0.0 all-reduce.17.cloned.1.call-start
  305.5 33.0 %all-gather.3 = bf16[8,10,4096]{2,1,0:T(8,128)(2,1)S(1)} all-gather(bf16[1,10,4096]{2,1,0:T(8,128)(2,1)S(1)} %get-tuple-element.12), channel_id=1, replica_groups=mesh['row'=8,'col'=4] {'row'}, dimensions={0}, use_global_device_ids=true | all-gather | bytes 737280 | tf_op jit(solution)/shard_map/all_gather | solution.py:80
  338.5 0.2 reshape.17
  338.7 6.0 %fusion.11 = f32[80,1024]{1,0:T(8,128)S(1)} fusion(bf16[80,4096]{1,0:T(8,128)(2,1)S(1)} %reshape.17, bf16[1024,4096]{1,0:T(8,128)(2,1)} %param.6), kind=kOutput, calls=%fused_computation.31 | convolution fusion | flops 671088640 | bytes 9371648 | tf_op jit(solution)/shard_map/dot_general | solution.py:89
  344.8 32.4 %all-gather.4 = bf16[8,10,4096]{2,1,0:T(8,128)(2,1)S(1)} all-gather(bf16[1,10,4096]{2,1,0:T(8,128)(2,1)S(1)} %get-tuple-element.11), channel_id=1, replica_groups=mesh['row'=8,'col'=4] {'row'}, dimensions={0}, use_global_device_ids=true | all-gather | bytes 737280 | tf_op jit(solution)/shard_map/all_gather | solution.py:81
  377.1 0.2 reshape.19
  377.4 6.8 %convolution_add_fusion = f32[80,1024]{1,0:T(8,128)} fusion(f32[80,1024]{1,0:T(8,128)S(1)} %fusion.11, bf16[80,4096]{1,0:T(8,128)(2,1)S(1)} %reshape.19, bf16[1024,4096]{1,0:T(8,128)(2,1)} %param.7), kind=kOutput, calls=%fused_computation.6 | convolution fusion | flops 671170560 | bytes 9699328 | tf_op jit(solution)/shard_map/dot_general | solution.py:91
  384.1 0.0 all-reduce.17.cloned.1.call-update
  384.2 5.8 %convolution_convert_fusion.2 = bf16[1024,4096]{1,0:T(8,128)(2,1)} fusion(bf16[80,1024]{1,0:T(8,128)(2,1)S(1)} %copy-done, bf16[80,4096]{1,0:T(8,128)(2,1)S(1)} %reshape.17), kind=kOutput, calls=%fused_computation.2 | convolution fusion | flops 675282944 | bytes 9207808 | tf_op jit(solution)/shard_map/dot_general | solution.py:83
  389.9 5.8 %convolution_convert_fusion.1 = bf16[1024,4096]{1,0:T(8,128)(2,1)} fusion(bf16[80,1024]{1,0:T(8,128)(2,1)S(1)} %copy-done, bf16[80,4096]{1,0:T(8,128)(2,1)S(1)} %reshape.19), kind=kOutput, calls=%fused_computation.1 | convolution fusion | flops 675282944 | bytes 9207808 | tf_op jit(solution)/shard_map/dot_general | solution.py:86
  395.7 0.0 all-reduce.13.cloned.1.call-done
  395.7 0.0 copy-start.1
  395.7 5.1 %fusion.9 = f32[80,2048]{1,0:T(8,128)S(1)} fusion(bf16[80,2048]{1,0:T(8,128)(2,1)} %all-reduce.13.cloned.1.call-done, bf16[2048,2048]{1,0:T(8,128)(2,1)} %param.8), kind=kOutput, calls=%fused_computation.29 | convolution fusion | flops 671088640 | bytes 9371648 | tf_op jit(solution)/shard_map/dot_general | solution.py:62
  400.8 14.9 %all-reduce.17.cloned.1.call-done = f32[80,1024]{1,0:T(8,128)} async-done(((f32[80,1024]{1,0:T(8,128)}), f32[80,1024]{1,0:T(8,128)}) %all-reduce.17.cloned.1.call-update) | async-done | bytes 327696 | tf_op jit(solution)/shard_map/psum | solution.py:37
  415.8 1.0 broadcast_select_fusion.2
  416.8 74.8 %all-reduce.20 = (bf16[80,2048]{1,0:T(8,128)(2,1)S(1)}, bf16[80,1024]{1,0:T(8,128)(2,1)S(1)}, bf16[80,1024]{1,0:T(8,128)(2,1)S(1)}) all-reduce(f32[80,2048]{1,0:T(8,128)S(1)} %fusion.9, f32[80,1024]{1,0:T(8,128)S(1)} %get-tuple-element.17, f32[80,1024]{1,0:T(8,128)S(1)} %get-tuple-element.16), channel_id=3, replica_groups=mesh['row'=8,'col'=4] {'row'}, use_global_device_ids=true, to_apply=%region_3.4.clone | all-reduce | flops 327680 | bytes 1966080
  491.6 0.7 fusion.5
  492.3 0.0 copy-done.1
  492.3 5.8 %convolution_convert_fusion = bf16[2048,2048]{1,0:T(8,128)(2,1)} fusion(bf16[80,2048]{1,0:T(8,128)(2,1)S(1)} %copy-done.1, bf16[80,2048]{1,0:T(8,128)(2,1)S(1)} %reshape.15), kind=kOutput, calls=%fused_computation | convolution fusion | flops 675282944 | bytes 9043968 | tf_op jit(solution)/shard_map/dot_general | solution.py:67
Async XLA Ops:
  7.2 72.8 %all-reduce.11.cloned.1.call-start = ((), (), s32[]{:S(2)}) async-start(), calls=%async_computation | async-start | bytes 327680 | tf_op jit(solution)/shard_map/psum | solution.py:12
  41.3 73.7 %all-reduce.15.cloned.1.call-start = ((), (), s32[]{:S(2)}) async-start(), calls=%async_computation.2 | async-start | bytes 1310720 | tf_op jit(solution)/shard_map/psum | solution.py:37
  79.9 190.1 %all-reduce.19.cloned.1.call-start = ((), (), s32[]{:S(2)}) async-start(), calls=%async_computation.4 | async-start | bytes 7864320
  80.0 5.1 %copy-start = (bf16[80,1024]{1,0:T(8,128)(2,1)S(1)}, bf16[80,1024]{1,0:T(8,128)(2,1)}, u32[]{:S(2)}) copy-start(bf16[80,1024]{1,0:T(8,128)(2,1)} %all-reduce.11.cloned.1.call-done) | copy-start | bytes 491524
  90.2 27.2 %copy-start.2 = (u32[32]{0:T(128)S(1)}, u32[32]{0:T(128)}, u32[]{:S(2)}) copy-start(u32[32]{0:T(128)} %constant.61) | copy-start | bytes 388
  117.3 278.4 %all-reduce.13.cloned.1.call-start = ((), (), s32[]{:S(2)}) async-start(), calls=%async_computation.1 | async-start | bytes 655360 | tf_op jit(solution)/shard_map/psum | solution.py:12
  305.4 110.3 %all-reduce.17.cloned.1.call-start = ((), (), s32[]{:S(2)}) async-start(), calls=%async_computation.3 | async-start | bytes 655360 | tf_op jit(solution)/shard_map/psum | solution.py:37
  395.7 96.6 %copy-start.1 = (bf16[80,2048]{1,0:T(8,128)(2,1)S(1)}, bf16[80,2048]{1,0:T(8,128)(2,1)}, u32[]{:S(2)}) copy-start(bf16[80,2048]{1,0:T(8,128)(2,1)} %all-reduce.13.cloned.1.call-done) | copy-start | bytes 983044
Sparse Core Ops, SparseCore 0:
  41.5 32.6 all-reduce.10
  80.0 34.9 all-reduce.14
  119.9 150.0 all-reduce.18
  305.6 31.1 all-reduce.12
  384.3 31.4 all-reduce.16
where the time goes:
time: 505 us
  blocking collectives  238 us (47%)
  waiting for transfers between devices  190 us (38%)
  matrix products  52.3 us (10%)
  between operations  14.6 us (3%)
  other arithmetic  8.79 us (2%)
    unnamed x6, waiting for transfers between devices  151 us
    unnamed x1, blocking collectives  74.8 us
    psum x2, waiting for transfers between devices, col_total(): return lax.psum(matrix, 'col')  38.1 us
    all_gather x1, blocking collectives, per_device(): lax.all_gather(tokens, 'row', axis=0, tiled=True)  33.2 us
    all_gather x1, blocking collectives, per_device(): lax.all_gather(gate_term, 'row', axis=0, tiled=True)  33 us
    all_gather x1, blocking collectives, per_device(): hidden_all = lax.all_gather(hidden_share, 'row', axis=0, tiled=True)  32.7 us
    all_gather x1, blocking collectives, per_device(): lax.all_gather(up_term, 'row', axis=0, tiled=True)  32.4 us
    all_gather x1, blocking collectives, per_device(): lax.all_gather(out_grad, 'row', axis=0, tiled=True)  31.5 us
  transfers between devices with their start and end apart: 5, of which 3 were waited for; matrix products, arithmetic and copies ran while one was open for 10% of the time, Pallas kernels for 0%

commit v1 on v0

--- a/solution.py
+++ b/solution.py
@@ -1,6 +1,11 @@
+import functools
+
 import jax
 import jax.numpy as jnp
+import numpy as np
 from jax import lax
+from jax.experimental import pallas as pl
+from jax.experimental.pallas import tpu as pltpu
 from jax.sharding import PartitionSpec as P
 
 rows_contract = (((0,), (0,)), ((), ()))
@@ -96,15 +101,384 @@
     return (output, grad_tokens, grad_gate, grad_up, grad_down)
 
 
+MESH = pl.DeviceIdType.MESH
+PAD = 16
+f32, bf16 = jnp.float32, jnp.bfloat16
+
+
+def mm(a, b):
+    return jnp.dot(a, b, preferred_element_type=f32)
+
+
+def mm_t(a, b):
+    return lax.dot_general(a, b, cols_contract, preferred_element_type=f32)
+
+
+def layer(
+    R, C,
+    tok, og, wg_hbm, wu_hbm, wd_hbm, ex,
+    out, gtok, toks, cot, hid, gg, ug,
+    wg, wu, wd, tokbuf, ogbuf, own, xsend, xrecv, zsend, zrecv, gupd,
+    ghsend, ghrecv, ghsum, ghfin, hsend, hbuf, tbuf, hex_, po, fxrecv, fzsend, fzrecv,
+    acc, grecv, gsum, gtbuf,
+    w_sem, tok_s, tok_r, og_s, og_r, x_s, x_r, z_s, z_r, gh_s, gh_r, gh2_s, gh2_r,
+    h_s, h_r, t_s, t_r, tf_s, fx_s, fx_r, fz_s, fz_r, g_s, g_r, g2_s, g2_r,
+):
+    r, c = lax.axis_index("row"), lax.axis_index("col")
+    H, Z = R // C, R // 2
+    z, x = r // 2, r % 2
+    mate = z * 2 + (1 - x)
+    S = wg.shape[1] // R
+    Dr = wg.shape[0]
+
+    def rc(src, dst, ss, rs, dr, dc):
+        return pltpu.make_async_remote_copy(
+            src_ref=src, dst_ref=dst, send_sem=ss, recv_sem=rs,
+            device_id=(dr, dc), device_id_type=MESH,
+        )
+
+    def start_any(src, dst, ss, rs, dr, dc):
+        here = jnp.logical_and(dr == r, dc == c)
+
+        @pl.when(jnp.logical_not(here))
+        def _():
+            rc(src, dst, ss, rs, dr, dc).start()
+
+        @pl.when(here)
+        def _():
+            pltpu.make_async_copy(src, dst, rs).start()
+
+    def sent_any(src, dst, ss, rs, dr, dc):
+        @pl.when(jnp.logical_not(jnp.logical_and(dr == r, dc == c)))
+        def _():
+            rc(src, dst, ss, rs, dr, dc).wait_send()
+
+    def arrived(dst, rs):
+        pltpu.make_async_copy(dst, dst, rs).wait()
+
+    def loop(n, body):
+        lax.fori_loop(0, n, lambda k, _: (body(k), 0)[1], 0)
+
+    def cols(k, n):
+        return pl.ds(pl.multiple_of(k * n, n), n)
+
+    loads = [
+        pltpu.make_async_copy(a, b, w_sem.at[i])
+        for i, (a, b) in enumerate(((wg_hbm, wg), (wu_hbm, wu), (wd_hbm, wd)))
+    ]
+    for load in loads:
+        load.start()
+
+    def tok_args(k):
+        h, c2 = k // C, (k + c) % C
+        return (
+            tok.at[:, cols(h, Dr)], tokbuf.at[cols(r, PAD)], tok_s.at[k], tok_r.at[r], c * H + h, c2
+        )
+
+    def og_args(k):
+        return (og, ogbuf.at[cols(r, PAD)], og_s.at[k], og_r.at[r], (r + k + 1) % R, c)
+
+    loop(R, lambda k: start_any(*tok_args(k)))
+    loop(R - 1, lambda k: rc(*og_args(k)).start())
+    ogbuf[cols(r, PAD), :] = og[...]
+    loop(R, lambda k: arrived(tokbuf.at[cols(k, PAD)], tok_r.at[k]))
+    toks[...] = lax.dot_general(
+        ex[...], tokbuf[...], rows_contract, preferred_element_type=f32
+    ).astype(bf16)
+
+    loads[0].wait()
+    loads[1].wait()
+
+    def x_args(k):
+        return (xsend.at[k], xrecv.at[k], x_s.at[k], x_r.at[k], mate, c)
+
+    def zp(k):
+        return (z + k + 1) % Z
+
+    def away(k):
+        zz = zp(k)
+        sub = zz * 2 + (1 - x)
+        xsend[zz, :, 0:S] = mm(toks[...], wg[:, cols(sub, S)]).astype(bf16)
+        xsend[zz, :, S : 2 * S] = mm(toks[...], wu[:, cols(sub, S)]).astype(bf16)
+        rc(*x_args(zz)).start()
+
+    loop(Z, away)
+
+    def home(k):
+        zz = zp(k)
+        sub = zz * 2 + x
+        own[zz, :, 0:S] = mm(toks[...], wg[:, cols(sub, S)])
+        own[zz, :, S : 2 * S] = mm(toks[...], wu[:, cols(sub, S)])
+
+    loop(Z, home)
+
+    def z_args(k):
+        return (zsend.at[zp(k)], zrecv.at[z], z_s.at[k], z_r.at[z], zp(k) * 2 + x, c)
+
+    def along(k):
+        zz = zp(k)
+        arrived(xrecv.at[zz], x_r.at[zz])
+        zsend[zz] = (own[zz] + xrecv[zz].astype(f32)).astype(bf16)
+        rc(*z_args(k)).start()
+
+    loop(Z - 1, along)
+
+    def og_wait(k):
+        src = (r + k + 1) % R
+        arrived(ogbuf.at[cols(src, PAD)], og_r.at[src])
+
+    loop(R - 1, og_wait)
+    cot[...] = lax.dot_general(
+        ex[...], ogbuf[...], rows_contract, preferred_element_type=f32
+    ).astype(bf16)
+    loads[2].wait()
+
+    def gh_args(k):
+        j = (c + k + 1) % C
+        return (ghsend.at[j], ghrecv.at[c], gh_s.at[k], gh_r.at[c], r, j)
+
+    def gh_step(k):
+        j = (c + k + 1) % C
+        ghsend[j] = mm_t(cot[...], wd[cols(j, S), :])
+        rc(*gh_args(k)).start()
+
+    loop(C - 1, gh_step)
+    ghsum[...] = mm_t(cot[...], wd[cols(c, S), :])
+    arrived(xrecv.at[z], x_r.at[z])
+    gupd[...] = own[z] + xrecv[z].astype(f32)
+
+    def gh_add(k):
+        j = (c + k + 1) % C
+        arrived(ghrecv.at[j], gh_r.at[j])
+        ghsum[...] += ghrecv[j]
+
+    loop(C - 1, gh_add)
+    mine = r * C + c
+    gh2 = (ghsum, ghfin, gh2_s.at[0], gh2_r.at[0], mine % R, mine // R)
+    start_any(*gh2)
+
+    def z_add(k):
+        zz = zp(k)
+        arrived(zrecv.at[zz], z_r.at[zz])
+        gupd[...] += zrecv[zz].astype(f32)
+
+    loop(Z - 1, z_add)
+    held = c * R + r
+    hsend[...] = (
+        gupd[:, 0:S] * jax.nn.sigmoid(gupd[:, 0:S]) * gupd[:, S : 2 * S]
+    ).astype(bf16)
+
+    def h_args(k):
+        return (
+            hsend, hbuf.at[held % C], h_s.at[k], h_r.at[held % C], held // C, (c + k) % C
+        )
+
+    loop(C, lambda k: start_any(*h_args(k)))
+
+    arrived(ghfin, gh2_r.at[0])
+    gate, up, grad = gupd[:, 0:S], gupd[:, S : 2 * S], ghfin[...]
+    sg = jax.nn.sigmoid(gate)
+    tbuf[r, :, 0:S] = (grad * up * sg * (1.0 + gate * (1.0 - sg))).astype(bf16)
+    tbuf[r, :, S : 2 * S] = (grad * (gate * sg)).astype(bf16)
+
+    def t_args(k):
+        return (tbuf.at[r], tbuf.at[r], t_s.at[k], t_r.at[r], zp(k) * 2 + x, c)
+
+    def tf_args(k):
+        slot = (z + k) % Z * 2 + x
+        return (tbuf.at[slot], tbuf.at[slot], tf_s.at[k], t_r.at[slot], mate, c)
+
+    loop(Z - 1, lambda k: rc(*t_args(k)).start())
+    rc(*tf_args(0)).start()
+
+    def h_use(k):
+        arrived(hbuf.at[k], h_r.at[k])
+        hid[:, cols(k, S)] = hbuf[k]
+        hex_[:, cols(k, S)] = mm(ex[...], hbuf[k]).astype(bf16)
+
+    loop(C, h_use)
+    tile = S
+
+    def po_step(k):
+        po[:, cols(k, tile)] = mm(hex_[...], wd[:, cols(k, tile)])
+
+    loop(po.shape[1] // tile, po_step)
+
+    def fx_args(k):
+        return (
+            po.at[cols(k * 2 + 1 - x, PAD)], fxrecv.at[k], fx_s.at[k], fx_r.at[k], mate, c
+        )
+
+    loop(Z, lambda k: rc(*fx_args(zp(k))).start())
+
+    acc[...] = jnp.zeros_like(acc)
+
+    def use(slot):
+        gg[:, cols(slot, S)] = tbuf[slot, :, 0:S]
+        ug[:, cols(slot, S)] = tbuf[slot, :, S : 2 * S]
+        wide = mm(ex[...], tbuf[slot]).astype(bf16)
+        acc[...] += mm_t(wide[:, 0:S], wg[:, cols(slot, S)]) + mm_t(
+            wide[:, S : 2 * S], wu[:, cols(slot, S)]
+        )
+
+    def near(k):
+        slot = (z + k) % Z * 2 + x
+
+        @pl.when(k > 0)
+        def _():
+            arrived(tbuf.at[slot], t_r.at[slot])
+            rc(*tf_args(k)).start()
+
+        use(slot)
+
+    loop(Z, near)
+
+    def fz_args(k):
+        return (fzsend.at[zp(k)], fzrecv.at[z], fz_s.at[k], fz_r.at[z], zp(k) * 2 + x, c)
+
+    def fz_step(k):
+        zz = zp(k)
+        arrived(fxrecv.at[zz], fx_r.at[zz])
+        fzsend[zz] = po[cols(zz * 2 + x, PAD), :] + fxrecv[zz]
+        rc(*fz_args(k)).start()
+
+    loop(Z - 1, fz_step)
+
+    def far(k):
+        slot = (z + k) % Z * 2 + 1 - x
+        arrived(tbuf.at[slot], t_r.at[slot])
+        use(slot)
+
+    loop(Z, far)
+
+    def g_args(k):
+        j = (c + k + 1) % C
+        return (acc.at[cols(j, PAD * H)], grecv.at[c], g_s.at[k], g_r.at[c], r, j)
+
+    loop(C - 1, lambda k: rc(*g_args(k)).start())
+
+    arrived(fxrecv.at[z], fx_r.at[z])
+    total = po[cols(r, PAD), :] + fxrecv[z]
+    for k in range(Z - 1):
+        arrived(fzrecv.at[zp(k)], fz_r.at[zp(k)])
+        total = total + fzrecv[zp(k)]
+    out[...] = total.astype(bf16)
+
+    part = acc[cols(c, PAD * H), :]
+    for k in range(C - 1):
+        j = (c + k + 1) % C
+        arrived(grecv.at[j], g_r.at[j])
+        part = part + grecv[j]
+    gsum[...] = part.astype(bf16)
+
+    def g2_args(k):
+        return (
+            gsum.at[cols(k, PAD)], gtbuf.at[r % H], g2_s.at[k], g2_r.at[r % H], c * H + k, r // H
+        )
+
+    loop(H, lambda k: start_any(*g2_args(k)))
+    for k in range(H):
+        arrived(gtbuf.at[k], g2_r.at[k])
+        gtok[:, k * Dr : (k + 1) * Dr] = gtbuf[k]
+
+    loop(R, lambda k: sent_any(*tok_args(k)))
+    loop(R - 1, lambda k: rc(*og_args(k)).wait_send())
+    loop(Z, lambda k: rc(*x_args(k)).wait_send())
+    loop(Z - 1, lambda k: rc(*z_args(k)).wait_send())
+    loop(C - 1, lambda k: rc(*gh_args(k)).wait_send())
+    sent_any(*gh2)
+    loop(C, lambda k: sent_any(*h_args(k)))
+    loop(Z - 1, lambda k: rc(*t_args(k)).wait_send())
+    loop(Z, lambda k: rc(*tf_args(k)).wait_send())
+    loop(Z, lambda k: rc(*fx_args(k)).wait_send())
+    loop(Z - 1, lambda k: rc(*fz_args(k)).wait_send())
+    loop(C - 1, lambda k: rc(*g_args(k)).wait_send())
+    loop(H, lambda k: sent_any(*g2_args(k)))
+
+
+def weight_grads(toks, gg, ug, hid, cot, dg, du, dd):
+    dg[...] = lax.dot_general(
+        toks[...], gg[...], rows_contract, preferred_element_type=f32
+    ).astype(bf16)
+    du[...] = lax.dot_general(
+        toks[...], ug[...], rows_contract, preferred_element_type=f32
+    ).astype(bf16)
+    dd[...] = lax.dot_general(
+        hid[...], cot[...], rows_contract, preferred_element_type=f32
+    ).astype(bf16)
+
+
+def per_device_kernels(R, C, tokens, w_gate, w_up, w_down, out_grad):
+    tr, dc = tokens.shape
+    T, Tp = tr * R, PAD * R
+    dr, fc = w_gate.shape
+    fr = w_down.shape[0]
+    S = fc // R
+    H, Z = R // C, R // 2
+    expand = np.zeros((Tp, T), np.float32)
+    for t in range(T):
+        expand[t // tr * PAD + t % tr, t] = 1.0
+    fill = ((0, PAD - tr), (0, 0))
+    vm, anym = pl.BlockSpec(memory_space=pltpu.VMEM), pl.BlockSpec(memory_space=pl.ANY)
+    shape = jax.ShapeDtypeStruct
+    sem = lambda *n: pltpu.SemaphoreType.DMA(n)
+    vmem = pltpu.VMEM
+    out, gtok, toks, cot, hid, gg, ug = pl.pallas_call(
+        functools.partial(layer, R, C),
+        out_shape=(
+            shape((PAD, dc), bf16), shape((PAD, dc), bf16), shape((T, dr), bf16),
+            shape((T, dc), bf16), shape((T, fr), bf16), shape((T, fc), bf16), shape((T, fc), bf16),
+        ),
+        in_specs=[vm, vm, anym, anym, anym, vm],
+        out_specs=(vm,) * 7,
+        scratch_shapes=[
+            vmem((dr, fc), bf16), vmem((dr, fc), bf16), vmem((fr, dc), bf16),
+            vmem((Tp, dr), bf16), vmem((Tp, dc), bf16),
+            vmem((Z, T, 2 * S), f32), vmem((Z, T, 2 * S), bf16), vmem((Z, T, 2 * S), bf16),
+            vmem((Z, T, 2 * S), bf16), vmem((Z, T, 2 * S), bf16), vmem((T, 2 * S), f32),
+            vmem((C, T, S), f32), vmem((C, T, S), f32), vmem((T, S), f32), vmem((T, S), f32),
+            vmem((T, S), bf16), vmem((C, T, S), bf16), vmem((R, T, 2 * S), bf16), vmem((Tp, fr), bf16),
+            vmem((Tp, dc), f32), vmem((Z, PAD, dc), f32), vmem((Z, PAD, dc), f32), vmem((Z, PAD, dc), f32),
+            vmem((Tp, dr), f32), vmem((C, PAD * H, dr), f32), vmem((PAD * H, dr), bf16), vmem((H, PAD, dr), bf16),
+            sem(3), sem(R), sem(R), sem(R), sem(R), sem(Z), sem(Z), sem(Z), sem(Z), sem(C), sem(C), sem(1), sem(1),
+            sem(C), sem(C), sem(Z), sem(R), sem(Z), sem(Z), sem(Z), sem(Z), sem(Z), sem(C), sem(C), sem(H), sem(H),
+        ],
+        compiler_params=pltpu.CompilerParams(
+            has_side_effects=True, vmem_limit_bytes=VMEM_LIMIT
+        ),
+    )(
+        jnp.pad(tokens, fill), jnp.pad(out_grad, fill), w_gate, w_up, w_down,
+        jnp.asarray(expand, bf16),
+    )
+    steps = 8
+    whole = lambda a: pl.BlockSpec(a.shape, lambda i: (0, 0))
+    part = lambda a: pl.BlockSpec((a.shape[0], a.shape[1] // steps), lambda i: (0, i))
+    block = lambda n, m: pl.BlockSpec((n // steps, m), lambda i: (i, 0))
+    dg, du, dd = pl.pallas_call(
+        weight_grads,
+        grid=(steps,),
+        out_shape=(shape((dr, fc), bf16), shape((dr, fc), bf16), shape((fr, dc), bf16)),
+        in_specs=[part(toks), whole(gg), whole(ug), part(hid), whole(cot)],
+        out_specs=(block(dr, fc), block(dr, fc), block(fr, dc)),
+        compiler_params=pltpu.CompilerParams(vmem_limit_bytes=VMEM_LIMIT),
+    )(toks, gg, ug, hid, cot)
+    return out[:tr], gtok[:tr], dg, du, dd
+
+
+VMEM_LIMIT = 52 * 1024 * 1024
+
+
 def solution(mesh):
-    in_specs = (P("row", "col"), P("row", "col"), P("row", "col"), P("row", "col"), P("row", "col"))
-    out_specs = (
-        P("row", "col"),
-        P("row", "col"),
-        P("row", "col"),
-        P("row", "col"),
-        P("row", "col"),
-    )
+    spec = P("row", "col")
+    R, C = mesh.shape["row"], mesh.shape["col"]
+
+    def run(tokens, w_gate, w_up, w_down, out_grad):
+        lanes = w_gate.shape[1] // R
+        aligned = lanes % 128 == 0 and w_gate.shape[0] % 1024 == 0 and tokens.shape[0] <= PAD
+        if aligned and R == 2 * C:
+            return per_device_kernels(R, C, tokens, w_gate, w_up, w_down, out_grad)
+        return per_device(tokens, w_gate, w_up, w_down, out_grad)
+
     return jax.shard_map(
-        per_device, mesh=mesh, in_specs=in_specs, out_specs=out_specs, check_vma=False
-    )
+        run, mesh=mesh, in_specs=(spec,) * 5, out_specs=(spec,) * 5, check_vma=False
+    )

time: 505 us -> 131 us (0.26)
  blocking collectives: 238 us -> 0 us
  waiting for transfers between devices: 190 us -> 0 us
  Pallas kernels: 0 us -> 125 us
  matrix products: 52.3 us -> 0 us
  between operations: 14.6 us -> 0.65 us
  other arithmetic: 8.79 us -> 0 us
    all_gather x5 -> x0, blocking collectives: 163 us -> none  [the longest x1 33.2 us: per_device(): lax.all_gather(tokens, 'row', axis=0, tiled=True)]
    unnamed x6 -> x0, waiting for transfers between devices: 151 us -> none
    pallas_call x0 -> x2, Pallas kernels: none -> 125 us  [the longest x1 114 us: per_device_kernels(): pl.pallas_call(functools.partial(layer, R, C), out_shape=(shape((PAD, dc)...]
    unnamed x1 -> x0, blocking collectives: 74.8 us -> none
    dot_general x9 -> x0, matrix products: 52.3 us -> none  [the longest x1 6.88 us: per_device(): lax.dot_general(cotangent_all, w_down, cols_contract, preferred_element_t...]
    psum x4 -> x0, waiting for transfers between devices: 38.1 us -> none  [the longest x2 38.1 us: col_total(): return lax.psum(matrix, 'col')]
  transfers between devices with their start and end apart: 5 -> 0, of which waited for: 3 -> 0; matrix products, arithmetic and copies ran while one was open for 10% -> 0% of each run, Pallas kernels for 0% -> 0%
where the time goes in v1:
time: 131 us; the launch traced here: 129 us
  Pallas kernels  125 us (95%)
  local copies, waits for them, and re-layouts  3.71 us (3%)
    pallas_call x1, Pallas kernels, per_device_kernels(): pl.pallas_call(functools.partial(layer, R, C), out_shape=(shape((PAD, dc)...  114 us
    pallas_call x1, Pallas kernels, per_device_kernels(): pl.pallas_call(weight_grads, grid=(steps,), out_shape=(shape((dr, fc), bf...  10.7 us

profile of v1, /device:TPU:0, one launch (start us, length us, event | category | flops | bytes accessed | tf_op | source)
XLA Modules:
  0.0 128.9 jit_solution(10279550427823550295)
XLA Ops:
  0.6 0.9 pad.7.tok
  1.5 0.8 pad.8.og
  2.3 0.0 copy-start
  2.3 0.8 copy-done
  3.1 113.8 %shard_map.101 = (bf16[16,2048]{1,0:T(8,128)(2,1)S(1)}, bf16[16,2048]{1,0:T(8,128)(2,1)S(1)}, bf16[80,1024]{1,0:T(8,128)(2,1)S(1)}, bf16[80,2048]{1,0:T(8,128)(2...) custom-call(bf16[16,2048]{1,0:T(8,128)(2,1)S(1)} %pad.7.tok, ...), custom_call_target="tpu_custom_call" | custom-call | tf_op jit(solution)/shard_map/pallas_call | solution.py:426
  116.9 10.7 %shard_map.102 = (bf16[1024,4096]{1,0:T(8,128)(2,1)}, bf16[1024,4096]{1,0:T(8,128)(2,1)}, bf16[2048,2048]{1,0:T(8,128)(2,1)}) custom-call(bf16[80,1024]{1,0:T(8,128)(2,1)S(1)} %get-tuple-element.17.toks, bf16[80,4096]{1,0:T(8,128)(2,1)S(1)} %get-tuple-element.18.gg, bf16[80,4096]{1,0:T(8,128)(2,1)} %get-tuple-element.19.ug, ...), custom_call_target="tpu_custom_call" | custom-call | tf_op jit(solution)/shard_map/pallas_call | solution.py:457
  127.7 0.6 copy.13
  128.3 0.6 copy.14
Async XLA Ops:
  2.3 0.8 copy-start

commit v2 on v1

--- a/solution.py
+++ b/solution.py
@@ -119,9 +119,9 @@
     tok, og, wg_hbm, wu_hbm, wd_hbm, ex,
     out, gtok, toks, cot, hid, gg, ug,
     wg, wu, wd, tokbuf, ogbuf, own, xsend, xrecv, zsend, zrecv, gupd,
-    ghsend, ghrecv, ghsum, ghfin, hsend, hbuf, tbuf, hex_, po, fxrecv, fzsend, fzrecv,
+    ghsend, ghrecv, ghsum, ghfin, hsend, hbuf, tbuf, hex_, po, fxsend, fxrecv, fzsend, fzrecv,
     acc, grecv, gsum, gtbuf,
-    w_sem, tok_s, tok_r, og_s, og_r, x_s, x_r, z_s, z_r, gh_s, gh_r, gh2_s, gh2_r,
+    w_sem, tok_s, tok2_s, tok_r, og_s, og2_s, og_r, x_s, x_r, z_s, z_r, gh_s, gh_r, gh2_s, gh2_r,
     h_s, h_r, t_s, t_r, tf_s, fx_s, fx_r, fz_s, fz_r, g_s, g_r, g2_s, g2_r,
 ):
     r, c = lax.axis_index("row"), lax.axis_index("col")
@@ -166,22 +166,63 @@
         pltpu.make_async_copy(a, b, w_sem.at[i])
         for i, (a, b) in enumerate(((wg_hbm, wg), (wu_hbm, wu), (wd_hbm, wd)))
     ]
-    for load in loads:
-        load.start()
-
-    def tok_args(k):
-        h, c2 = k // C, (k + c) % C
+    loads[0].start()
+    loads[1].start()
+    barrier = pltpu.get_barrier_semaphore()
+
+    def greet(k):
+        other = (r * C + c + k + 1) % (R * C)
+        pl.semaphore_signal(
+            barrier, inc=1, device_id=(other // C, other % C), device_id_type=MESH
+        )
+
+    loop(R * C - 1, greet)
+    pl.semaphore_wait(barrier, R * C - 1)
+
+    def zp(k):
+        return (z + k + 1) % Z
+
+    def tok_args(h):
         return (
-            tok.at[:, cols(h, Dr)], tokbuf.at[cols(r, PAD)], tok_s.at[k], tok_r.at[r], c * H + h, c2
+            tok.at[:, cols(h, Dr)], tokbuf.at[cols(r, PAD)], tok_s.at[h], tok_r.at[r],
+            c * H + h, r % C,
         )
 
+    def tok2_args(i):
+        src = c + i // (C - 1) * C
+        slot = tokbuf.at[cols(src, PAD)]
+        return (slot, slot, tok2_s.at[i], tok_r.at[src], r, (c + i % (C - 1) + 1) % C)
+
     def og_args(k):
-        return (og, ogbuf.at[cols(r, PAD)], og_s.at[k], og_r.at[r], (r + k + 1) % R, c)
-
-    loop(R, lambda k: start_any(*tok_args(k)))
-    loop(R - 1, lambda k: rc(*og_args(k)).start())
+        return (og, ogbuf.at[cols(r, PAD)], og_s.at[k], og_r.at[r], zp(k) * 2 + x, c)
+
+    def og2_args(k):
+        src = (z + k) % Z * 2 + x
+        slot = ogbuf.at[cols(src, PAD)]
+        return (slot, slot, og2_s.at[k], og_r.at[src], mate, c)
+
+    def og_own():
+        return (og, ogbuf.at[cols(r, PAD)], og2_s.at[0], og_r.at[r], mate, c)
+
+    loop(H, lambda h: start_any(*tok_args(h)))
+    loop(Z - 1, lambda k: rc(*og_args(k)).start())
+    rc(*og_own()).start()
+    loads[2].start()
     ogbuf[cols(r, PAD), :] = og[...]
-    loop(R, lambda k: arrived(tokbuf.at[cols(k, PAD)], tok_r.at[k]))
+
+    def tok_pass(m):
+        src = c + m * C
+        arrived(tokbuf.at[cols(src, PAD)], tok_r.at[src])
+        loop(C - 1, lambda k: rc(*tok2_args(m * (C - 1) + k)).start())
+
+    loop(H, tok_pass)
+
+    def tok_wait(k):
+        @pl.when(k % C != c)
+        def _():
+            arrived(tokbuf.at[cols(k, PAD)], tok_r.at[k])
+
+    loop(R, tok_wait)
     toks[...] = lax.dot_general(
         ex[...], tokbuf[...], rows_contract, preferred_element_type=f32
     ).astype(bf16)
@@ -191,9 +232,6 @@
 
     def x_args(k):
         return (xsend.at[k], xrecv.at[k], x_s.at[k], x_r.at[k], mate, c)
-
-    def zp(k):
-        return (z + k + 1) % Z
 
     def away(k):
         zz = zp(k)
@@ -202,6 +240,12 @@
         xsend[zz, :, S : 2 * S] = mm(toks[...], wu[:, cols(sub, S)]).astype(bf16)
         rc(*x_args(zz)).start()
 
+        @pl.when(k > 0)
+        def _():
+            src = (z + k) % Z * 2 + x
+            arrived(ogbuf.at[cols(src, PAD)], og_r.at[src])
+            rc(*og2_args(k)).start()
+
     loop(Z, away)
 
     def home(k):
@@ -210,8 +254,6 @@
         own[zz, :, 0:S] = mm(toks[...], wg[:, cols(sub, S)])
         own[zz, :, S : 2 * S] = mm(toks[...], wu[:, cols(sub, S)])
 
-    loop(Z, home)
-
     def z_args(k):
         return (zsend.at[zp(k)], zrecv.at[z], z_s.at[k], z_r.at[z], zp(k) * 2 + x, c)
 
@@ -221,13 +263,14 @@
         zsend[zz] = (own[zz] + xrecv[zz].astype(f32)).astype(bf16)
         rc(*z_args(k)).start()
 
-    loop(Z - 1, along)
+    home(0)
+    along(0)
 
     def og_wait(k):
-        src = (r + k + 1) % R
+        src = (z + k) % Z * 2 + 1 - x
         arrived(ogbuf.at[cols(src, PAD)], og_r.at[src])
 
-    loop(R - 1, og_wait)
+    loop(Z, og_wait)
     cot[...] = lax.dot_general(
         ex[...], ogbuf[...], rows_contract, preferred_element_type=f32
     ).astype(bf16)
@@ -242,7 +285,15 @@
         ghsend[j] = mm_t(cot[...], wd[cols(j, S), :])
         rc(*gh_args(k)).start()
 
-    loop(C - 1, gh_step)
+    gh_step(0)
+
+    def turn(k):
+        home(k + 1)
+        along(k + 1)
+        gh_step(k + 1)
+
+    loop(Z - 2, turn)
+    home(Z - 1)
     ghsum[...] = mm_t(cot[...], wd[cols(c, S), :])
     arrived(xrecv.at[z], x_r.at[z])
     gupd[...] = own[z] + xrecv[z].astype(f32)
@@ -268,12 +319,11 @@
         gupd[:, 0:S] * jax.nn.sigmoid(gupd[:, 0:S]) * gupd[:, S : 2 * S]
     ).astype(bf16)
 
+    h1 = (hsend, hbuf.at[held % C], h_s.at[0], h_r.at[held % C], held // C, held % C)
+    start_any(*h1)
+
     def h_args(k):
-        return (
-            hsend, hbuf.at[held % C], h_s.at[k], h_r.at[held % C], held // C, (c + k) % C
-        )
-
-    loop(C, lambda k: start_any(*h_args(k)))
+        return (hbuf.at[c], hbuf.at[c], h_s.at[k], h_r.at[c], r, (c + k) % C)
 
     arrived(ghfin, gh2_r.at[0])
     gate, up, grad = gupd[:, 0:S], gupd[:, S : 2 * S], ghfin[...]
@@ -291,10 +341,18 @@
     loop(Z - 1, lambda k: rc(*t_args(k)).start())
     rc(*tf_args(0)).start()
 
+    arrived(hbuf.at[c], h_r.at[c])
+    loop(C - 1, lambda k: rc(*h_args(k + 1)).start())
+
     def h_use(k):
-        arrived(hbuf.at[k], h_r.at[k])
-        hid[:, cols(k, S)] = hbuf[k]
-        hex_[:, cols(k, S)] = mm(ex[...], hbuf[k]).astype(bf16)
+        j = (c + k) % C
+
+        @pl.when(k > 0)
+        def _():
+            arrived(hbuf.at[j], h_r.at[j])
+
+        hid[:, cols(j, S)] = hbuf[j]
+        hex_[:, cols(j, S)] = mm(ex[...], hbuf[j]).astype(bf16)
 
     loop(C, h_use)
     tile = S
@@ -304,9 +362,14 @@
 
     loop(po.shape[1] // tile, po_step)
 
+    def fx_cast(k):
+        fxsend[k] = po[cols(k * 2 + 1 - x, PAD), :].astype(bf16)
+
+    loop(Z, fx_cast)
+
     def fx_args(k):
         return (
-            po.at[cols(k * 2 + 1 - x, PAD)], fxrecv.at[k], fx_s.at[k], fx_r.at[k], mate, c
+            fxsend.at[k], fxrecv.at[k], fx_s.at[k], fx_r.at[k], mate, c
         )
 
     loop(Z, lambda k: rc(*fx_args(zp(k))).start())
@@ -339,7 +402,7 @@
     def fz_step(k):
         zz = zp(k)
         arrived(fxrecv.at[zz], fx_r.at[zz])
-        fzsend[zz] = po[cols(zz * 2 + x, PAD), :] + fxrecv[zz]
+        fzsend[zz] = (po[cols(zz * 2 + x, PAD), :] + fxrecv[zz].astype(f32)).astype(bf16)
         rc(*fz_args(k)).start()
 
     loop(Z - 1, fz_step)
@@ -358,10 +421,10 @@
     loop(C - 1, lambda k: rc(*g_args(k)).start())
 
     arrived(fxrecv.at[z], fx_r.at[z])
-    total = po[cols(r, PAD), :] + fxrecv[z]
+    total = po[cols(r, PAD), :] + fxrecv[z].astype(f32)
     for k in range(Z - 1):
         arrived(fzrecv.at[zp(k)], fz_r.at[zp(k)])
-        total = total + fzrecv[zp(k)]
+        total = total + fzrecv[zp(k)].astype(f32)
     out[...] = total.astype(bf16)
 
     part = acc[cols(c, PAD * H), :]
@@ -381,13 +444,17 @@
         arrived(gtbuf.at[k], g2_r.at[k])
         gtok[:, k * Dr : (k + 1) * Dr] = gtbuf[k]
 
-    loop(R, lambda k: sent_any(*tok_args(k)))
-    loop(R - 1, lambda k: rc(*og_args(k)).wait_send())
+    loop(H, lambda h: sent_any(*tok_args(h)))
+    loop(H * (C - 1), lambda i: rc(*tok2_args(i)).wait_send())
+    loop(Z - 1, lambda k: rc(*og_args(k)).wait_send())
+    rc(*og_own()).wait_send()
+    loop(Z - 1, lambda k: rc(*og2_args(k + 1)).wait_send())
     loop(Z, lambda k: rc(*x_args(k)).wait_send())
     loop(Z - 1, lambda k: rc(*z_args(k)).wait_send())
     loop(C - 1, lambda k: rc(*gh_args(k)).wait_send())
     sent_any(*gh2)
-    loop(C, lambda k: sent_any(*h_args(k)))
+    sent_any(*h1)
+    loop(C - 1, lambda k: rc(*h_args(k + 1)).wait_send())
     loop(Z - 1, lambda k: rc(*t_args(k)).wait_send())
     loop(Z, lambda k: rc(*tf_args(k)).wait_send())
     loop(Z, lambda k: rc(*fx_args(k)).wait_send())
@@ -438,13 +505,14 @@
             vmem((Z, T, 2 * S), bf16), vmem((Z, T, 2 * S), bf16), vmem((T, 2 * S), f32),
             vmem((C, T, S), f32), vmem((C, T, S), f32), vmem((T, S), f32), vmem((T, S), f32),
             vmem((T, S), bf16), vmem((C, T, S), bf16), vmem((R, T, 2 * S), bf16), vmem((Tp, fr), bf16),
-            vmem((Tp, dc), f32), vmem((Z, PAD, dc), f32), vmem((Z, PAD, dc), f32), vmem((Z, PAD, dc), f32),
+            vmem((Tp, dc), f32), vmem((Z, PAD, dc), bf16), vmem((Z, PAD, dc), bf16),
+            vmem((Z, PAD, dc), bf16), vmem((Z, PAD, dc), bf16),
             vmem((Tp, dr), f32), vmem((C, PAD * H, dr), f32), vmem((PAD * H, dr), bf16), vmem((H, PAD, dr), bf16),
-            sem(3), sem(R), sem(R), sem(R), sem(R), sem(Z), sem(Z), sem(Z), sem(Z), sem(C), sem(C), sem(1), sem(1),
+            sem(3), sem(H), sem(H * (C - 1)), sem(R), sem(Z), sem(Z), sem(R), sem(Z), sem(Z), sem(Z), sem(Z), sem(C), sem(C), sem(1), sem(1),
             sem(C), sem(C), sem(Z), sem(R), sem(Z), sem(Z), sem(Z), sem(Z), sem(Z), sem(C), sem(C), sem(H), sem(H),
         ],
         compiler_params=pltpu.CompilerParams(
-            has_side_effects=True, vmem_limit_bytes=VMEM_LIMIT
+            collective_id=0, has_side_effects=True, vmem_limit_bytes=VMEM_LIMIT
         ),
     )(
         jnp.pad(tokens, fill), jnp.pad(out_grad, fill), w_gate, w_up, w_down,

time: 131 us -> 119 us (0.908)
  the two profiles are of different devices: /device:TPU:0 before, /device:TPU:15 now
where the time goes in v2:
time: 119 us; the launch traced here: 118 us
  Pallas kernels  114 us (96%)
  local copies, waits for them, and re-layouts  3.71 us (3%)
    pallas_call x1, Pallas kernels, per_device_kernels(): pl.pallas_call(functools.partial(layer, R, C), out_shape=(shape((PAD, dc)...  103 us
    pallas_call x1, Pallas kernels, per_device_kernels(): pl.pallas_call(weight_grads, grid=(steps,), out_shape=(shape((dr, fc), bf...  10.7 us

profile of v2, /device:TPU:15, one launch (start us, length us, event | category | flops | bytes accessed | tf_op | source)
XLA Modules:
  0.0 118.4 jit_solution(2594454556605158284)
XLA Ops:
  0.6 0.9 pad.7.tok
  1.5 0.8 pad.8.og
  2.3 0.0 copy-start
  2.3 0.8 copy-done
  3.1 103.3 %shard_map.101 = (bf16[16,2048]{1,0:T(8,128)(2,1)S(1)}, bf16[16,2048]{1,0:T(8,128)(2,1)S(1)}, bf16[80,1024]{1,0:T(8,128)(2,1)S(1)}, bf16[80,2048]{1,0:T(8,128)(2...) custom-call(bf16[16,2048]{1,0:T(8,128)(2,1)S(1)} %pad.7.tok, ...), custom_call_target="tpu_custom_call" | custom-call | tf_op jit(solution)/shard_map/pallas_call | solution.py:493
  106.4 10.7 %shard_map.102 = (bf16[1024,4096]{1,0:T(8,128)(2,1)}, bf16[1024,4096]{1,0:T(8,128)(2,1)}, bf16[2048,2048]{1,0:T(8,128)(2,1)}) custom-call(bf16[80,1024]{1,0:T(8,128)(2,1)S(1)} %get-tuple-element.17.toks, bf16[80,4096]{1,0:T(8,128)(2,1)S(1)} %get-tuple-element.18.gg, bf16[80,4096]{1,0:T(8,128)(2,1)} %get-tuple-element.19.ug, ...), custom_call_target="tpu_custom_call" | custom-call | tf_op jit(solution)/shard_map/pallas_call | solution.py:525
  117.1 0.6 copy.13
  117.8 0.6 copy.14
Async XLA Ops:
  2.3 0.8 copy-start
